TPU v7x, 128 devices: a whole 4x4x4 slice. The times are simulated.
128 devices in a mesh: seq: 16 (over y_hi, z, core), tp: 8 (over y_lo, x).
Axes of the slice: x: 4, y: 4 (y_hi: 2, y_lo: 2; y = y_hi * 2 + y_lo), z: 4, core: 2. Of those that a mesh axis runs over, the one named last changes fastest.
Arguments:
- queries: bfloat16 [8192, 4096], P('seq', 'tp'), may hold values from -6 to 6
- keys: bfloat16 [8192, 4096], P('seq', 'tp'), may hold values from -6 to 6
- values: bfloat16 [8192, 4096], P('seq', 'tp'), may hold values from -16 to 16
- offsets: int32 [3, 32], replicated, may hold values from 0 to 7, as said below
- out_weight: bfloat16 [4096, 4096], P('tp'), may hold values from -0.09375 to 0.09375
- out_grad: bfloat16 [8192, 4096], P('seq', 'tp'), may hold values from -6 to 6
Outputs:
- result: bfloat16 [8192, 4096], P('seq', 'tp')
- grad_queries: bfloat16 [8192, 4096], P('seq', 'tp')
- grad_keys: bfloat16 [8192, 4096], P('seq', 'tp')
- grad_values: bfloat16 [8192, 4096], P('seq', 'tp')
- grad_weight: bfloat16 [4096, 4096], P('tp', 'seq')
Inputs may be any that keep to these rules, and one draw needn't show every extreme that they name: offsets[j, h] is below 2^(j+1).
All inputs are finite; a program needn't handle non-finite values.
Results may differ from a plain program's by a relative error of at most 0.023.
Values may be sent and summed in bfloat16 or wider, within the bound.
A program may use at most 128 MiB of HBM per device.

v0:
```python
import jax
import jax.numpy as jnp
from jax import lax
from jax.experimental import pallas as pl
from jax.experimental.pallas import tpu as pltpu
from jax.sharding import PartitionSpec as P

DH = 128
LEV = 3
R = 512
C = 512
HL = 4
SCALE = DH**-0.5
K2E = SCALE * 1.4426950408889634
NEG = -1e30
BF = jnp.bfloat16
F32 = jnp.float32

NAMES = (
    ["og1", "og3", "ogA", "ogB", "w", "wf"]
    + ["kvo1", "kvo2", "kvo3", "kv2", "kvf2"]
    + ["kv3_1", "kv3_2", "kv3_3", "kvf3_1", "kvf3_2", "kvf3_3"]
    + ["att0", "att1", "att2", "att3", "g"]
    + ["ra", "rb", "r1", "r3"]
    + ["%s%d" % (name, hb) for hb in range(2) for name in ("gcA", "gcB", "za", "zb", "z1", "z3")]
    + ["y0", "y1", "c1", "c2", "c3", "b2_1", "b3_1", "b3_2", "b3_3"]
)
ID = {name: i for i, name in enumerate(NAMES)}


def dot(a, b):
    return lax.dot_general(a, b, (((1,), (0,)), ((), ())), preferred_element_type=F32)


def dot_t(a, b):
    return lax.dot_general(a, b, (((1,), (1,)), ((), ())), preferred_element_type=F32)


def heads(body):
    for h in range(HL):
        body(h)


def loop(count, body):
    def step(i, carry):
        body(i)
        return carry

    lax.fori_loop(0, count, step, 0)


def kernel(
    offs, q_hbm, k_hbm, v_hbm, w_hbm, og_hbm,
    res_o, dq_o, dk_o, dv_o, gw_o,
    stage, perm, unperm, eye, qp, kp, vp, kv1, kv2, kv3, e0, e1, e2, e3, mm0, mm1, mm2, mm3,
    m_run, l_run, n_run, attp, att_buf, att_t, og_buf, wblk, g_own, g_send, g_recv, gp,
    res_s, res_a, res_b, res_r, res_f, gc_s, gc_r, gz_s, gz_a, gz_b, gz_r, gz_f, gy_s, gy_r,
    dqa, dk0, dv0, snd1, snd2, snd3, cr1, cr2, cr3, zs2, zs3, rz2, rz3, back,
    ss, rs, ls,
):
    s = lax.axis_index("seq")
    t = lax.axis_index("tp")
    core = s % 2
    z = (s // 2) % 4
    yh = s // 8
    x = t % 4
    q = t // 4
    y = 2 * yh + q
    s_base = yh * 8
    s8 = s % 8
    kv = [None, kv1, kv2, kv3]
    es = [e0, e1, e2, e3]
    mms = [mm0, mm1, mm2, mm3]
    snd = [None, snd1, snd2, snd3]
    sent = []

    def to_seq(mask):
        return (s_base + (s8 ^ mask), t)

    def to_x(mask):
        return (s, q * 4 + (x ^ mask))

    def to_y(yy):
        return ((yy // 2) * 8 + s8, (yy % 2) * 4 + x)

    def remote(src, dst, name, device, extra=0):
        i = ID[name] + extra
        return pltpu.make_async_remote_copy(
            src_ref=src, dst_ref=dst, send_sem=ss.at[i], recv_sem=rs.at[i],
            device_id=device, device_id_type=pl.DeviceIdType.MESH,
        )

    def send(src, dst, name, device):
        copy = remote(src, dst, name, device)
        copy.start()
        sent.append(copy)

    def arrived(dst, name):
        remote(dst, dst, name, to_seq(1)).wait_recv()

    def head_cols(h):
        return pl.ds(h * DH, DH)

    def local(src, dst, i):
        copy = pltpu.make_async_copy(src, dst, ls.at[i])
        copy.start()
        return copy

    barrier = pltpu.get_barrier_semaphore()
    peers = [to_seq(m) for m in range(1, 8)] + [to_x(1), to_x(3)] + [to_y((y + d) % 4) for d in (1, 2, 3)]
    for peer in peers:
        pl.semaphore_signal(barrier, inc=1, device_id=peer, device_id_type=pl.DeviceIdType.MESH)
    k_in = local(k_hbm, stage.at[0], 0)
    v_in = local(v_hbm, stage.at[1], 1)
    q_in = local(q_hbm, stage.at[2], 2)
    og_in = local(og_hbm, og_buf.at[x], 3)
    half = pl.ds(pl.multiple_of(q * 2048, 2048), 2048)
    w_in = local(w_hbm.at[:, half], wblk.at[q], 4)


    def place_of(i):
        return ((i & 1) << 8) | (((i >> 1) & 1) << 7) | (((i >> 2) & 1) << 6) | (i >> 3)

    rows_i = lax.broadcasted_iota(jnp.int32, (R, R), 0)
    cols_i = lax.broadcasted_iota(jnp.int32, (R, R), 1)
    perm[...] = jnp.where(rows_i == place_of(cols_i), 1.0, 0.0).astype(BF)
    pl.semaphore_wait(barrier, len(peers))

    send(og_hbm, og_buf.at[x], "og1", to_x(1))
    send(og_hbm, og_buf.at[x], "og3", to_x(3))
    w_there = pl.ds(pl.multiple_of((1 - q) * 2048 + core * 1024, 1024), 1024)
    w_mine = pl.ds(pl.multiple_of(core * 1024, 1024), 1024)
    w_other = pl.ds(pl.multiple_of((1 - core) * 1024, 1024), 1024)
    send(w_hbm.at[:, w_there], wblk.at[q, :, w_mine], "w", to_y((y + 3 + 2 * core) % 4))

    def permuted(src, dst):
        def tile(b):
            rows = pl.ds(pl.multiple_of(b * 256, 256), 256)
            moved = dot(perm[rows, :], src[...]).astype(BF)
            for h in range(HL):
                dst[h, rows, :] = moved[:, h * DH : (h + 1) * DH]

        loop(2, tile)

    def phase_of(level, h):
        return offs[level - 1, t * HL + h]

    def chosen(value, level, h):
        for bit in range(level):
            n = value.shape[0] // 2
            flag = jnp.full((n, DH), (phase_of(level, h) >> bit) & 1, jnp.int32)
            value = jnp.where(flag == 1, value[n:], value[:n])
        return value

    def chosen_bf(value, level, h):
        return value if level == 0 else chosen(value.astype(F32), level, h).astype(BF)

    unperm[...] = jnp.where(cols_i == place_of(rows_i), 1.0, 0.0).astype(BF)
    eye[...] = jnp.where(rows_i == cols_i, 1.0, 0.0).astype(BF)
    k_in.wait()
    permuted(stage.at[0], kp)
    v_in.wait()
    permuted(stage.at[1], vp)
    for level in (3, 2, 1):
        n = R >> level
        slot = s % (1 << level)

        def fill(h, level=level, n=n, slot=slot):
            kv[level][slot, :, head_cols(h)] = chosen_bf(kp[h], level, h)
            kv[level][slot, :, head_cols(h + HL)] = chosen_bf(vp[h], level, h)

        heads(fill)
        mine = kv[level].at[slot]
        if level == 3:
            for m in (2, 1, 3):
                send(mine, mine, "kv3_%d" % m, to_seq(2 * m))
        if level == 2:
            send(mine, mine, "kv2", to_seq(2))
        send(mine, mine, "kvo%d" % level, to_seq(1))
    q_in.wait()
    permuted(stage.at[2], qp)

    def placed(value, level, h, fill):
        phase = jnp.full(value.shape, phase_of(level, h), jnp.int32)
        order = [sum(((p >> (level - 1 - bit)) & 1) << bit for bit in range(level)) for p in range(1 << level)]
        return jnp.concatenate([jnp.where(phase == p, value, fill) for p in order], axis=0)

    def keys_of(level, h, which):
        if level == 0:
            return (kp, vp)[which][h]
        return kv[level][:, :, head_cols(h + HL * which)].reshape(R, DH)

    def forward(level, h):
        n = R >> level
        rows = min(n, 256)
        keys = keys_of(level, h, 0)
        vals = jnp.concatenate([keys_of(level, h, 1), jnp.ones((R, DH), BF)], axis=1)
        for b in range(0, n, rows):
            if level == 0:
                queries = qp[h, b : b + rows, :]
            else:
                queries = chosen_bf(qp[h], level, h)
            scores = dot_t(queries, keys) * K2E
            top = jnp.max(scores, axis=1, keepdims=True)
            e = jnp.exp2(scores - top).astype(BF)
            es[level][h, b : b + rows, :] = e
            nl = dot(e, vals)
            top = jnp.broadcast_to(top, (rows, DH))
            mms[level][h, b : b + rows, :] = top
            if level == 0:
                m_run[h, b : b + rows, :] = top
                n_run[h, b : b + rows, :] = nl[:, :DH]
                l_run[h, b : b + rows, :] = nl[:, DH:]
        if level > 0:
            old = m_run[h]
            this = placed(top, level, h, NEG)
            new = jnp.maximum(old, this)
            a_old = jnp.exp2(old - new)
            a_this = jnp.exp2(this - new)
            m_run[h] = new
            n_run[h] = n_run[h] * a_old + a_this * jnp.concatenate([nl[:, :DH]] * (1 << level), axis=0)
            l_run[h] = l_run[h] * a_old + a_this * jnp.concatenate([nl[:, DH:]] * (1 << level), axis=0)

    heads(lambda h: forward(0, h))

    s4 = s % 4
    there = kv2.at[s4 ^ 2]
    arrived(there, "kv2")
    send(there, there, "kvf2", to_seq(1))
    arrived(kv1.at[core ^ 1], "kvo1")
    heads(lambda h: forward(1, h))
    for m in (1, 3, 2):
        there = kv3.at[s8 ^ (2 * m)]
        arrived(there, "kv3_%d" % m)
        send(there, there, "kvf3_%d" % m, to_seq(1))
    arrived(kv2.at[s4 ^ 1], "kvo2")
    arrived(kv2.at[s4 ^ 3], "kvf2")
    arrived(og_buf.at[x ^ 1], "og1")
    send(og_buf.at[x ^ 1, 0:256], og_buf.at[x ^ 1, 0:256], "ogA", to_x(3))
    arrived(og_buf.at[x ^ 3], "og3")
    send(og_buf.at[x ^ 3, 256:512], og_buf.at[x ^ 3, 256:512], "ogB", to_x(1))
    w_got = wblk.at[1 - q, :, w_mine]
    arrived(w_got, "w")
    send(w_got, w_got, "wf", to_seq(1))

    heads(lambda h: forward(2, h))

    arrived(kv3.at[s8 ^ 1], "kvo3")
    for m in (1, 3, 2):
        arrived(kv3.at[s8 ^ (2 * m + 1)], "kvf3_%d" % m)

    def last_level(h):
        forward(3, h)
        inverse = 1.0 / l_run[h]
        l_run[h] = inverse
        attended = (n_run[h] * inverse).astype(BF)
        attp[h] = attended
        att_buf[q, :, head_cols(h)] = dot(unperm[...], attended).astype(BF)
        block = att_buf.at[q, :, head_cols(h)]
        remote(block, block, "att0", to_y(y ^ 1), extra=h).start()

    heads(last_level)
    for h in range(HL):
        block = att_buf.at[q, :, h * DH : (h + 1) * DH]
        sent.append(remote(block, block, "att%d" % h, to_y(y ^ 1)))

    og_in.wait()
    w_in.wait()
    arrived(og_buf.at[x ^ 2, 0:256], "ogA")
    arrived(og_buf.at[x ^ 2, 256:512], "ogB")
    arrived(wblk.at[1 - q, :, w_other], "wf")

    def grad_part(which, dst):
        def tile(b):
            rows = pl.ds(pl.multiple_of(b * 256, 256), 256)
            total = dot_t(og_buf[0, rows, :], wblk[which, :, 0:512])
            for xx in range(1, 4):
                total += dot_t(og_buf[xx, rows, :], wblk[which, :, xx * 512 : (xx + 1) * 512])
            dst[rows, :] = total.astype(dst.dtype)

        loop(2, tile)

    grad_part(1 - q, g_send)
    send(g_send, g_recv, "g", to_y(y ^ 1))

    order = (2, 3, 1, 0)

    def transposed(hb, which):
        for h in range(HL):
            att_t[hb, h * DH : (h + 1) * DH, :] = dot_t(eye[:DH, :DH], att_buf[which, :, h * DH : (h + 1) * DH]).astype(BF)

    def weight_part(hb, i, cc):
        cols = pl.ds(pl.multiple_of(cc * 256, 256), 256)
        return dot(att_t[hb], og_buf[z ^ order[i], :, cols])

    def weight_first(hb):
        for i in range(4):
            gc_s[hb, i] = weight_part(hb, i, 1 - core).astype(BF)
            if i == 0:
                send(gc_s.at[hb, 0], gc_r.at[hb, 0], "gcA%d" % hb, to_seq(1))
        send(gc_s.at[hb, 1:4], gc_r.at[hb, 1:4], "gcB%d" % hb, to_seq(1))

    def weight_second(hb):
        arrived(gc_r.at[hb, 0], "gcA%d" % hb)
        gz_s[hb, 0] = (weight_part(hb, 0, core) + gc_r[hb, 0].astype(F32)).astype(BF)
        send(gz_s.at[hb, 0, 0:256], gz_a.at[hb], "za%d" % hb, to_seq(2))
        send(gz_s.at[hb, 0, 256:512], gz_b.at[hb], "zb%d" % hb, to_seq(6))
        arrived(gc_r.at[hb, 1:4], "gcB%d" % hb)
        for i in range(1, 4):
            gz_f[hb, i - 1] = weight_part(hb, i, core) + gc_r[hb, i].astype(F32)

    def weight_third(hb):
        arrived(gz_a.at[hb], "za%d" % hb)
        gz_s[hb, 1, 0:256, :] = (gz_f[hb, 0, 0:256, :] + gz_a[hb].astype(F32)).astype(BF)
        gz_s[hb, 1, 256:512, :] = gz_f[hb, 0, 256:512, :].astype(BF)
        send(gz_s.at[hb, 1], gz_r.at[hb, 1], "z3%d" % hb, to_seq(6))
        arrived(gz_b.at[hb], "zb%d" % hb)
        gz_s[hb, 2, 0:256, :] = gz_f[hb, 1, 0:256, :].astype(BF)
        gz_s[hb, 2, 256:512, :] = (gz_f[hb, 1, 256:512, :] + gz_b[hb].astype(F32)).astype(BF)
        send(gz_s.at[hb, 2], gz_r.at[hb, 0], "z1%d" % hb, to_seq(2))

    def last_hop(hb):
        i = ID["y0"]
        return pltpu.make_async_remote_copy(
            src_ref=gy_s.at[hb], dst_ref=gy_r.at[yh], send_sem=ss.at[i + hb], recv_sem=rs.at[i + yh],
            device_id=to_y(3 * q if hb == 0 else q + 1), device_id_type=pl.DeviceIdType.MESH,
        )

    def weight_fourth(hb):
        arrived(gz_r.at[hb, 0], "z1%d" % hb)
        arrived(gz_r.at[hb, 1], "z3%d" % hb)
        total = gz_f[hb, 2] + gz_r[hb, 0].astype(F32) + gz_r[hb, 1].astype(F32)
        gy_s[hb] = total.astype(BF)
        if hb == 1:
            last_hop(1).start()
            return

        @pl.when(yh == q)
        def _():
            gy_r[yh] = gy_s[0]

        @pl.when(yh != q)
        def _():
            last_hop(0).start()

    def result_part(i):
        cols = pl.ds(pl.multiple_of((x ^ order[i]) * 512, 512), 512)
        return dot(att_buf[0], wblk[0, :, cols]) + dot(att_buf[1], wblk[1, :, cols])

    transposed(0, q)
    weight_first(0)
    grad_part(q, g_own)
    weight_second(0)

    for h in range(HL):
        arrived(att_buf.at[1 - q, :, h * DH : (h + 1) * DH], "att%d" % h)
    res_s[0] = result_part(0).astype(BF)
    send(res_s.at[0, 0:256], res_a, "ra", to_x(1))
    send(res_s.at[0, 256:512], res_b, "rb", to_x(3))
    transposed(1, 1 - q)
    weight_first(1)
    for i in range(1, 4):
        res_f[i - 1] = result_part(i)
    weight_third(0)
    weight_second(1)
    arrived(res_a, "ra")
    res_s[1, 0:256, :] = (res_f[0, 0:256, :] + res_a[...].astype(F32)).astype(BF)
    res_s[1, 256:512, :] = res_f[0, 256:512, :].astype(BF)
    send(res_s.at[1], res_r.at[1], "r3", to_x(3))
    arrived(res_b, "rb")
    res_s[2, 0:256, :] = res_f[1, 0:256, :].astype(BF)
    res_s[2, 256:512, :] = (res_f[1, 256:512, :] + res_b[...].astype(F32)).astype(BF)
    send(res_s.at[2], res_r.at[0], "r1", to_x(1))
    weight_third(1)

    arrived(g_recv, "g")

    def grad_total(b):
        rows = pl.ds(pl.multiple_of(b * 256, 256), 256)
        stage[0, rows, :] = (g_own[rows, :] + g_recv[rows, :].astype(F32)).astype(BF)

    loop(2, grad_total)
    permuted(stage.at[0], gp)

    def backward(level, h):
        n = R >> level
        keys = keys_of(level, h, 0)
        vals = keys_of(level, h, 1)
        grads = chosen(gp[h].astype(F32), level, h)
        factor = jnp.exp2(mms[level][h] - chosen(m_run[h], level, h)) * chosen(l_run[h], level, h)
        scaled = grads * factor
        delta = jnp.sum(scaled * chosen(attp[h].astype(F32), level, h), axis=1, keepdims=True)
        scaled = scaled.astype(BF)
        e = es[level][h]
        ds = (e.astype(F32) * (dot_t(scaled, vals) - delta)).astype(BF)
        dq = dot(ds, keys) * SCALE
        if level == 0:
            dqa[h] += dq
        elif level == 3:
            dqa[h] = placed(dq, level, h, 0.0)
        else:
            dqa[h] += placed(dq, level, h, 0.0)
        scaled_t = dot_t(eye[:DH, :DH], scaled).astype(BF)
        query_t = dot_t(eye[:DH, :DH], chosen_bf(qp[h], level, h)).astype(BF)
        dv_t = dot(scaled_t, e)
        dk_t = dot(query_t, ds) * SCALE
        both = dot_t(eye[...], jnp.concatenate([dk_t, dv_t], axis=0).astype(BF))
        if level == 0:
            dk0[h] = both[:, :DH]
            dv0[h] = both[:, DH:]
        else:
            shape = snd[level].shape[:-1] + (DH,)
            snd[level][..., head_cols(h)] = both[:, :DH].astype(BF).reshape(shape)
            snd[level][..., head_cols(h + HL)] = both[:, DH:].astype(BF).reshape(shape)

    zb = z % 2
    heads(lambda h: backward(3, h))
    send(snd3.at[:, 1 - core], cr3, "c3", to_seq(1))
    heads(lambda h: backward(2, h))
    send(snd2.at[:, 1 - core], cr2, "c2", to_seq(1))
    arrived(cr3, "c3")
    for m in (2, 1, 3):
        zs3[m - 1] = (snd3[z ^ m, core].astype(F32) + cr3[z ^ m].astype(F32)).astype(BF)
        send(zs3.at[m - 1], rz3.at[m - 1], "b3_%d" % m, to_seq(2 * m))
    heads(lambda h: backward(1, h))
    send(snd1.at[1 - core], cr1, "c1", to_seq(1))
    arrived(cr2, "c2")
    zs2[...] = (snd2[zb ^ 1, core].astype(F32) + cr2[zb ^ 1].astype(F32)).astype(BF)
    send(zs2, rz2, "b2_1", to_seq(2))
    weight_fourth(0)
    heads(lambda h: backward(0, h))

    def natural(dst):
        def tile(b):
            rows = pl.ds(pl.multiple_of(b * 256, 256), 256)
            dst[rows, :] = dot(unperm[rows, :], back[...]).astype(BF)

        loop(2, tile)

    for h in range(HL):
        back[:, h * DH : (h + 1) * DH] = dqa[h].astype(BF)
    natural(dq_o)

    arrived(res_r.at[0], "r1")
    arrived(res_r.at[1], "r3")

    def result_total(b):
        rows = pl.ds(pl.multiple_of(b * 128, 128), 128)
        res_o[rows, :] = (res_f[2, rows, :] + res_r[0, rows, :].astype(F32) + res_r[1, rows, :].astype(F32)).astype(BF)

    loop(4, result_total)
    weight_fourth(1)

    arrived(cr1, "c1")
    for m in (1, 3, 2):
        arrived(rz3.at[m - 1], "b3_%d" % m)
    arrived(rz2, "b2_1")

    for which, start_grad, dst in ((0, dk0, dk_o), (1, dv0, dv_o)):

        def key_total(h, which=which, start_grad=start_grad):
            total = start_grad[h]
            cols = head_cols(h + HL * which)
            owed = snd1[core, :, cols].astype(F32) + cr1[:, cols].astype(F32)
            total += placed(owed, 1, h, 0.0)
            owed = snd2[zb, core, :, cols].astype(F32) + cr2[zb, :, cols].astype(F32) + rz2[:, cols].astype(F32)
            total += placed(owed, 2, h, 0.0)
            owed = snd3[z, core, :, cols].astype(F32) + cr3[z, :, cols].astype(F32)
            for m in range(3):
                owed += rz3[m, :, cols].astype(F32)
            total += placed(owed, 3, h, 0.0)
            back[:, head_cols(h)] = total.astype(BF)

        heads(key_total)
        natural(dst)

    for source in range(2):

        @pl.when(jnp.logical_not((yh == source) & (q == yh)))
        def _(source=source):
            arrived(gy_r.at[source], "y%d" % source)

    gw_o[...] = (gy_r[0].astype(F32) + gy_r[1].astype(F32)).astype(BF)

    last_hop(1).wait_send()

    @pl.when(yh != q)
    def _():
        last_hop(0).wait_send()

    for copy in sent:
        copy.wait_send()


def hand_over(*refs):
    sources, targets, held, sems = refs[:5], refs[5:10], refs[10:15], refs[15]
    reads = [pltpu.make_async_copy(sources[i], held[i], sems.at[0, i]) for i in range(5)]
    writes = [pltpu.make_async_copy(held[i], targets[i], sems.at[1, i]) for i in range(5)]
    for copy in reads:
        copy.start()
    for i in range(5):
        reads[i].wait()
        writes[i].start()
    for copy in writes:
        copy.wait()


def shards(queries, keys, values, offsets, out_weight, out_grad):
    wide = jax.ShapeDtypeStruct((R, C), BF)
    any_spec = pl.BlockSpec(memory_space=pl.ANY)
    vmem = pl.BlockSpec(memory_space=pltpu.VMEM)

    def bf(*shape):
        return pltpu.VMEM(shape, BF)

    def f32(*shape):
        return pltpu.VMEM(shape, F32)

    count = len(NAMES)
    outs = (wide, wide, wide, wide, jax.ShapeDtypeStruct((512, 256), BF))
    made = pl.pallas_call(
        kernel,
        out_shape=outs,
        in_specs=[pl.BlockSpec(memory_space=pltpu.SMEM)] + [any_spec] * 5,
        out_specs=[vmem] * 5,
        scratch_shapes=[
            bf(3, R, C), bf(R, R), bf(R, R), bf(R, R),
            bf(HL, R, DH), bf(HL, R, DH), bf(HL, R, DH),
            bf(2, 256, 1024), bf(4, 128, 1024), bf(8, 64, 1024),
            bf(HL, 512, R), bf(HL, 256, R), bf(HL, 128, R), bf(HL, 64, R),
            f32(HL, 512, DH), f32(HL, 256, DH), f32(HL, 128, DH), f32(HL, 64, DH),
            f32(HL, R, DH), f32(HL, R, DH), f32(HL, R, DH),
            bf(HL, R, DH), bf(2, R, C), bf(2, C, R),
            bf(4, R, C), bf(2, C, 2048),
            f32(R, C), bf(R, C), bf(R, C), bf(HL, R, DH),
            bf(3, R, C), bf(256, C), bf(256, C), bf(2, R, C), f32(3, R, C),
            bf(2, 4, C, 256), bf(2, 4, C, 256),
            bf(2, 3, C, 256), bf(2, 256, 256), bf(2, 256, 256), bf(2, 2, C, 256), f32(2, 3, C, 256),
            bf(2, 512, 256), bf(2, 512, 256),
            f32(HL, R, DH), f32(HL, R, DH), f32(HL, R, DH),
            bf(2, 256, 1024), bf(2, 2, 128, 1024), bf(4, 2, 64, 1024),
            bf(256, 1024), bf(2, 128, 1024), bf(4, 64, 1024),
            bf(128, 1024), bf(3, 64, 1024), bf(128, 1024), bf(3, 64, 1024),
            bf(R, C),
            pltpu.SemaphoreType.DMA((count,)), pltpu.SemaphoreType.DMA((count,)), pltpu.SemaphoreType.DMA((5,)),
        ],
        compiler_params=pltpu.CompilerParams(
            collective_id=0, has_side_effects=True, vmem_limit_bytes=60 * 1024 * 1024
        ),
    )(offsets, queries, keys, values, out_weight, out_grad)
    return pl.pallas_call(
        hand_over, out_shape=outs, in_specs=[any_spec] * 5, out_specs=[any_spec] * 5,
        scratch_shapes=[pltpu.VMEM(out.shape, BF) for out in outs] + [pltpu.SemaphoreType.DMA((2, 5))],
        compiler_params=pltpu.CompilerParams(vmem_limit_bytes=60 * 1024 * 1024),
    )(*made)


def solution(mesh):
    return jax.shard_map(
        shards,
        mesh=mesh,
        in_specs=(
            P("seq", "tp"),
            P("seq", "tp"),
            P("seq", "tp"),
            P(),
            P("tp", None),
            P("seq", "tp"),
        ),
        out_specs=(P("seq", "tp"), P("seq", "tp"), P("seq", "tp"), P("seq", "tp"), P("tp", "seq")),
        check_vma=False,
    )
```

profile of v0, /device:TPU:8, one launch (start us, length us, event | category | flops | bytes accessed | tf_op | source)
XLA Modules:
  0.0 78.0 jit_solution(10842712945231162915)
XLA Ops:
  0.6 74.7 %shard_map.101 = (bf16[512,512]{1,0:T(8,128)(2,1)}, bf16[512,512]{1,0:T(8,128)(2,1)}, bf16[512,512]{1,0:T(8,128)(2,1)}, bf16[512,512]{1,0:T(8,128)(2,1)}, bf16[512,256]{1,0:T(8,128)(2,1)}) custom-call(s32[3,32]{1,0:T(4,128)} %offs.1, bf16[512,512]{1,0:T(8,128)(2,1)} %q_hbm.1, bf16[512,512]{1,0:T(8,128)(2,1)} %k_hbm.1, bf16[512,512]{1,0:T(8,128)(2,1)} %v_hbm.1, ...), custom_call_target="tpu_custom_call" | custom-call | tf_op jit(solution)/shard_map/pallas_call | solution.py:521
  75.3 2.5 %shard_map.102 = (bf16[512,512]{1,0:T(8,128)(2,1)}, bf16[512,512]{1,0:T(8,128)(2,1)}, bf16[512,512]{1,0:T(8,128)(2,1)}, bf16[512,512]{1,0:T(8,128)(2,1)}, bf16[512,256]{1,0:T(8,128)(2,1)}) custom-call(bf16[512,512]{1,0:T(8,128)(2,1)} %get-tuple-element.10.refs_0_, bf16[512,512]{1,0:T(8,128)(2,1)} %get-tuple-element.11.refs_1_, ...), custom_call_target="tpu_custom_call" | custom-call | tf_op jit(solution)/shard_map/pallas_call | solution.py:551
where the time goes:
time: 78.4 us; the launch traced here: 78 us
  Pallas kernels  77.2 us (98%)
  between operations  0.82 us (1%)
    pallas_call x1, Pallas kernels, shards(): pl.pallas_call(kernel, out_shape=outs, in_specs=[pl.BlockSpec(memory_spac...  74.7 us
    pallas_call x1, Pallas kernels, shards(): pl.pallas_call(hand_over, out_shape=outs, in_specs=[any_spec] * 5, out_sp...  2.52 us

commit v1 on v0

--- a/solution.py
+++ b/solution.py
@@ -17,13 +17,14 @@
 F32 = jnp.float32
 
 NAMES = (
-    ["og1", "og3", "ogA", "ogB", "w", "wf"]
+    ["og1a", "og1b", "og3a", "og3b", "ogA", "ogB", "w", "wf"]
     + ["kvo1", "kvo2", "kvo3", "kv2", "kvf2"]
-    + ["kv3_1", "kv3_2", "kv3_3", "kvf3_1", "kvf3_2", "kvf3_3"]
-    + ["att0", "att1", "att2", "att3", "g"]
-    + ["ra", "rb", "r1", "r3"]
-    + ["%s%d" % (name, hb) for hb in range(2) for name in ("gcA", "gcB", "za", "zb", "z1", "z3")]
-    + ["y0", "y1", "c1", "c2", "c3", "b2_1", "b3_1", "b3_2", "b3_3"]
+    + ["kv3_1", "kv3_3", "kv3A", "kv3B", "kvf3_1", "kvf3_3", "kvf3_2"]
+    + ["att0", "att1", "g0", "g1"]
+    + ["ra", "rb", "r1a", "r1b", "r3a", "r3b"]
+    + ["%s%d" % (name, hb) for hb in range(2) for name in ("gcA", "gcB", "za", "zb", "z1a", "z1b", "z3a", "z3b")]
+    + ["y0", "y1"]
+    + ["%s_%d" % (name, hp) for hp in range(2) for name in ("c1", "c2", "c3", "b2_1", "b3_1", "b3_2", "b3_3")]
 )
 ID = {name: i for i, name in enumerate(NAMES)}
 
@@ -54,8 +55,8 @@
     res_o, dq_o, dk_o, dv_o, gw_o,
     stage, perm, unperm, eye, qp, kp, vp, kv1, kv2, kv3, e0, e1, e2, e3, mm0, mm1, mm2, mm3,
     m_run, l_run, n_run, attp, att_buf, att_t, og_buf, wblk, g_own, g_send, g_recv, gp,
-    res_s, res_a, res_b, res_r, res_f, gc_s, gc_r, gz_s, gz_a, gz_b, gz_r, gz_f, gy_s, gy_r,
-    dqa, dk0, dv0, snd1, snd2, snd3, cr1, cr2, cr3, zs2, zs3, rz2, rz3, back,
+    res_s, res_a, res_b, res_r, res_f, gc_s, gc_r, gz_s, gz_a, gz_b, gz_r, gz_f, gz_t, gy_s, gy_r,
+    dqa, dk0, dv0, snd1, snd2, snd3, cr1, cr2, cr3, zs2, zs3, rz2, rz3, back, qt0, qt1, qt2, qt3,
     ss, rs, ls,
 ):
     s = lax.axis_index("seq")
@@ -72,7 +73,8 @@
     es = [e0, e1, e2, e3]
     mms = [mm0, mm1, mm2, mm3]
     snd = [None, snd1, snd2, snd3]
-    sent = []
+    qts = [qt0, qt1, qt2, qt3]
+    sent = {}
 
     def to_seq(mask):
         return (s_base + (s8 ^ mask), t)
@@ -93,7 +95,10 @@
     def send(src, dst, name, device):
         copy = remote(src, dst, name, device)
         copy.start()
-        sent.append(copy)
+        sent[name] = copy
+
+    def left(name):
+        sent.pop(name).wait_send()
 
     def arrived(dst, name):
         remote(dst, dst, name, to_seq(1)).wait_recv()
@@ -124,14 +129,6 @@
     rows_i = lax.broadcasted_iota(jnp.int32, (R, R), 0)
     cols_i = lax.broadcasted_iota(jnp.int32, (R, R), 1)
     perm[...] = jnp.where(rows_i == place_of(cols_i), 1.0, 0.0).astype(BF)
-    pl.semaphore_wait(barrier, len(peers))
-
-    send(og_hbm, og_buf.at[x], "og1", to_x(1))
-    send(og_hbm, og_buf.at[x], "og3", to_x(3))
-    w_there = pl.ds(pl.multiple_of((1 - q) * 2048 + core * 1024, 1024), 1024)
-    w_mine = pl.ds(pl.multiple_of(core * 1024, 1024), 1024)
-    w_other = pl.ds(pl.multiple_of((1 - core) * 1024, 1024), 1024)
-    send(w_hbm.at[:, w_there], wblk.at[q, :, w_mine], "w", to_y((y + 3 + 2 * core) % 4))
 
     def permuted(src, dst):
         def tile(b):
@@ -155,8 +152,6 @@
     def chosen_bf(value, level, h):
         return value if level == 0 else chosen(value.astype(F32), level, h).astype(BF)
 
-    unperm[...] = jnp.where(cols_i == place_of(rows_i), 1.0, 0.0).astype(BF)
-    eye[...] = jnp.where(rows_i == cols_i, 1.0, 0.0).astype(BF)
     k_in.wait()
     permuted(stage.at[0], kp)
     v_in.wait()
@@ -170,13 +165,28 @@
             kv[level][slot, :, head_cols(h + HL)] = chosen_bf(vp[h], level, h)
 
         heads(fill)
-        mine = kv[level].at[slot]
-        if level == 3:
-            for m in (2, 1, 3):
-                send(mine, mine, "kv3_%d" % m, to_seq(2 * m))
-        if level == 2:
-            send(mine, mine, "kv2", to_seq(2))
-        send(mine, mine, "kvo%d" % level, to_seq(1))
+
+    pl.semaphore_wait(barrier, len(peers))
+    w_there = pl.ds(pl.multiple_of((1 - q) * 2048 + core * 1024, 1024), 1024)
+    w_mine = pl.ds(pl.multiple_of(core * 1024, 1024), 1024)
+    w_other = pl.ds(pl.multiple_of((1 - core) * 1024, 1024), 1024)
+
+    def send_grads(name, rows, mask):
+        send(og_hbm.at[rows : rows + 256], og_buf.at[x, rows : rows + 256], name, to_x(mask))
+
+    mine = [kv[level].at[s % (1 << level)] if level else None for level in range(4)]
+    send(mine[3], mine[3], "kv3_1", to_seq(2))
+    send(mine[3], mine[3], "kv3_3", to_seq(6))
+    send(mine[2], mine[2], "kv2", to_seq(2))
+    send_grads("og1a", 0, 1)
+    send_grads("og3b", 256, 3)
+    send_grads("og1b", 256, 1)
+    send_grads("og3a", 0, 3)
+    send(w_hbm.at[:, w_there], wblk.at[q, :, w_mine], "w", to_y((y + 3 + 2 * core) % 4))
+    for level in (1, 2, 3):
+        send(mine[level], mine[level], "kvo%d" % level, to_seq(1))
+    unperm[...] = jnp.where(cols_i == place_of(rows_i), 1.0, 0.0).astype(BF)
+    eye[...] = jnp.where(rows_i == cols_i, 1.0, 0.0).astype(BF)
     q_in.wait()
     permuted(stage.at[2], qp)
 
@@ -223,28 +233,33 @@
 
     heads(lambda h: forward(0, h))
 
+    arrived(kv1.at[core ^ 1], "kvo1")
+    heads(lambda h: forward(1, h))
+
     s4 = s % 4
+    for m, half_at in ((1, 0), (3, 1)):
+        there = kv3.at[s8 ^ (2 * m)]
+        arrived(there, "kv3_%d" % m)
+        part = kv3.at[s8 ^ (2 * m), half_at * 32 : half_at * 32 + 32]
+        send(part, part, ("kv3A", "kv3B")[half_at], to_seq(2 * (4 - m)))
+        send(there, there, "kvf3_%d" % m, to_seq(1))
+    arrived(og_buf.at[x ^ 1, 0:256], "og1a")
+    send(og_buf.at[x ^ 1, 0:256], og_buf.at[x ^ 1, 0:256], "ogA", to_x(3))
+    arrived(og_buf.at[x ^ 3, 256:512], "og3b")
+    send(og_buf.at[x ^ 3, 256:512], og_buf.at[x ^ 3, 256:512], "ogB", to_x(1))
     there = kv2.at[s4 ^ 2]
     arrived(there, "kv2")
     send(there, there, "kvf2", to_seq(1))
-    arrived(kv1.at[core ^ 1], "kvo1")
-    heads(lambda h: forward(1, h))
-    for m in (1, 3, 2):
-        there = kv3.at[s8 ^ (2 * m)]
-        arrived(there, "kv3_%d" % m)
-        send(there, there, "kvf3_%d" % m, to_seq(1))
-    arrived(kv2.at[s4 ^ 1], "kvo2")
-    arrived(kv2.at[s4 ^ 3], "kvf2")
-    arrived(og_buf.at[x ^ 1], "og1")
-    send(og_buf.at[x ^ 1, 0:256], og_buf.at[x ^ 1, 0:256], "ogA", to_x(3))
-    arrived(og_buf.at[x ^ 3], "og3")
-    send(og_buf.at[x ^ 3, 256:512], og_buf.at[x ^ 3, 256:512], "ogB", to_x(1))
+    arrived(kv3.at[s8 ^ 4, 0:32], "kv3A")
+    arrived(kv3.at[s8 ^ 4, 32:64], "kv3B")
+    there = kv3.at[s8 ^ 4]
+    send(there, there, "kvf3_2", to_seq(1))
     w_got = wblk.at[1 - q, :, w_mine]
     arrived(w_got, "w")
     send(w_got, w_got, "wf", to_seq(1))
-
+    arrived(kv2.at[s4 ^ 1], "kvo2")
+    arrived(kv2.at[s4 ^ 3], "kvf2")
     heads(lambda h: forward(2, h))
-
     arrived(kv3.at[s8 ^ 1], "kvo3")
     for m in (1, 3, 2):
         arrived(kv3.at[s8 ^ (2 * m + 1)], "kvf3_%d" % m)
@@ -256,32 +271,40 @@
         attended = (n_run[h] * inverse).astype(BF)
         attp[h] = attended
         att_buf[q, :, head_cols(h)] = dot(unperm[...], attended).astype(BF)
-        block = att_buf.at[q, :, head_cols(h)]
-        remote(block, block, "att0", to_y(y ^ 1), extra=h).start()
 
     heads(last_level)
-    for h in range(HL):
-        block = att_buf.at[q, :, h * DH : (h + 1) * DH]
-        sent.append(remote(block, block, "att%d" % h, to_y(y ^ 1)))
+
+    def send_attended(rh):
+        block = att_buf.at[q, rh * 256 : (rh + 1) * 256]
+        send(block, block, "att%d" % rh, to_y(y ^ 1))
+
+    send_attended(0)
+    send_attended(1)
+    for level in range(4):
+        for h in range(HL):
+            mms[level][h] = jnp.exp2(mms[level][h] - chosen(m_run[h], level, h)) * chosen(l_run[h], level, h)
+            qts[level][h] = dot_t(eye[:DH, :DH], chosen_bf(qp[h], level, h)).astype(BF)
 
     og_in.wait()
     w_in.wait()
+    arrived(og_buf.at[x ^ 1, 256:512], "og1b")
+    arrived(og_buf.at[x ^ 3, 0:256], "og3a")
     arrived(og_buf.at[x ^ 2, 0:256], "ogA")
     arrived(og_buf.at[x ^ 2, 256:512], "ogB")
     arrived(wblk.at[1 - q, :, w_other], "wf")
 
-    def grad_part(which, dst):
-        def tile(b):
-            rows = pl.ds(pl.multiple_of(b * 256, 256), 256)
-            total = dot_t(og_buf[0, rows, :], wblk[which, :, 0:512])
-            for xx in range(1, 4):
-                total += dot_t(og_buf[xx, rows, :], wblk[which, :, xx * 512 : (xx + 1) * 512])
-            dst[rows, :] = total.astype(dst.dtype)
-
-        loop(2, tile)
-
-    grad_part(1 - q, g_send)
-    send(g_send, g_recv, "g", to_y(y ^ 1))
+    def grad_part(which, dst, hp):
+        feats = slice(hp * 256, hp * 256 + 256)
+        total = dot_t(og_buf[0], wblk[which, feats, 0:512])
+        for xx in range(1, 4):
+            total += dot_t(og_buf[xx], wblk[which, feats, xx * 512 : (xx + 1) * 512])
+        dst[hp] = total.astype(dst.dtype)
+
+    def send_grad(hp):
+        send(g_send.at[hp], g_recv.at[hp], "g%d" % hp, to_y(y ^ 1))
+
+    grad_part(1 - q, g_send, 0)
+    grad_part(1 - q, g_send, 1)
 
     order = (2, 3, 1, 0)
 
@@ -306,18 +329,23 @@
         send(gz_s.at[hb, 0, 0:256], gz_a.at[hb], "za%d" % hb, to_seq(2))
         send(gz_s.at[hb, 0, 256:512], gz_b.at[hb], "zb%d" % hb, to_seq(6))
         arrived(gc_r.at[hb, 1:4], "gcB%d" % hb)
-        for i in range(1, 4):
-            gz_f[hb, i - 1] = weight_part(hb, i, core) + gc_r[hb, i].astype(F32)
+        part = weight_part(hb, 1, core) + gc_r[hb, 1].astype(F32)
+        gz_f[hb, 0] = part[0:256]
+        gz_s[hb, 1, 256:512, :] = part[256:512].astype(BF)
+        send(gz_s.at[hb, 1, 256:512], gz_r.at[hb, 1, 256:512], "z3b%d" % hb, to_seq(6))
+        part = weight_part(hb, 2, core) + gc_r[hb, 2].astype(F32)
+        gz_f[hb, 1] = part[256:512]
+        gz_s[hb, 2, 0:256, :] = part[0:256].astype(BF)
+        send(gz_s.at[hb, 2, 0:256], gz_r.at[hb, 0, 0:256], "z1a%d" % hb, to_seq(2))
+        gz_t[hb] = weight_part(hb, 3, core) + gc_r[hb, 3].astype(F32)
 
     def weight_third(hb):
         arrived(gz_a.at[hb], "za%d" % hb)
-        gz_s[hb, 1, 0:256, :] = (gz_f[hb, 0, 0:256, :] + gz_a[hb].astype(F32)).astype(BF)
-        gz_s[hb, 1, 256:512, :] = gz_f[hb, 0, 256:512, :].astype(BF)
-        send(gz_s.at[hb, 1], gz_r.at[hb, 1], "z3%d" % hb, to_seq(6))
+        gz_s[hb, 1, 0:256, :] = (gz_f[hb, 0] + gz_a[hb].astype(F32)).astype(BF)
+        send(gz_s.at[hb, 1, 0:256], gz_r.at[hb, 1, 0:256], "z3a%d" % hb, to_seq(6))
         arrived(gz_b.at[hb], "zb%d" % hb)
-        gz_s[hb, 2, 0:256, :] = gz_f[hb, 1, 0:256, :].astype(BF)
-        gz_s[hb, 2, 256:512, :] = (gz_f[hb, 1, 256:512, :] + gz_b[hb].astype(F32)).astype(BF)
-        send(gz_s.at[hb, 2], gz_r.at[hb, 0], "z1%d" % hb, to_seq(2))
+        gz_s[hb, 2, 256:512, :] = (gz_f[hb, 1] + gz_b[hb].astype(F32)).astype(BF)
+        send(gz_s.at[hb, 2, 256:512], gz_r.at[hb, 0, 256:512], "z1b%d" % hb, to_seq(2))
 
     def last_hop(hb):
         i = ID["y0"]
@@ -327,9 +355,10 @@
         )
 
     def weight_fourth(hb):
-        arrived(gz_r.at[hb, 0], "z1%d" % hb)
-        arrived(gz_r.at[hb, 1], "z3%d" % hb)
-        total = gz_f[hb, 2] + gz_r[hb, 0].astype(F32) + gz_r[hb, 1].astype(F32)
+        for rh, name in ((0, "z%da%d"), (1, "z%db%d")):
+            arrived(gz_r.at[hb, 0, rh * 256 : rh * 256 + 256], name % (1, hb))
+            arrived(gz_r.at[hb, 1, rh * 256 : rh * 256 + 256], name % (3, hb))
+        total = gz_t[hb] + gz_r[hb, 0].astype(F32) + gz_r[hb, 1].astype(F32)
         gy_s[hb] = total.astype(BF)
         if hb == 1:
             last_hop(1).start()
@@ -343,52 +372,69 @@
         def _():
             last_hop(0).start()
 
-    def result_part(i):
+    def result_part(i, rh):
+        rows = slice(rh * 256, rh * 256 + 256)
         cols = pl.ds(pl.multiple_of((x ^ order[i]) * 512, 512), 512)
-        return dot(att_buf[0], wblk[0, :, cols]) + dot(att_buf[1], wblk[1, :, cols])
+        return dot(att_buf[0, rows, :], wblk[0, :, cols]) + dot(att_buf[1, rows, :], wblk[1, :, cols])
 
     transposed(0, q)
     weight_first(0)
-    grad_part(q, g_own)
+    grad_part(q, g_own, 0)
+    grad_part(q, g_own, 1)
     weight_second(0)
 
-    for h in range(HL):
-        arrived(att_buf.at[1 - q, :, h * DH : (h + 1) * DH], "att%d" % h)
-    res_s[0] = result_part(0).astype(BF)
+    arrived(att_buf.at[1 - q, 0:256], "att0")
+    res_s[0, 0:256, :] = result_part(0, 0).astype(BF)
     send(res_s.at[0, 0:256], res_a, "ra", to_x(1))
-    send(res_s.at[0, 256:512], res_b, "rb", to_x(3))
-    transposed(1, 1 - q)
-    weight_first(1)
-    for i in range(1, 4):
-        res_f[i - 1] = result_part(i)
-    weight_third(0)
-    weight_second(1)
-    arrived(res_a, "ra")
-    res_s[1, 0:256, :] = (res_f[0, 0:256, :] + res_a[...].astype(F32)).astype(BF)
-    res_s[1, 256:512, :] = res_f[0, 256:512, :].astype(BF)
-    send(res_s.at[1], res_r.at[1], "r3", to_x(3))
-    arrived(res_b, "rb")
-    res_s[2, 0:256, :] = res_f[1, 0:256, :].astype(BF)
-    res_s[2, 256:512, :] = (res_f[1, 256:512, :] + res_b[...].astype(F32)).astype(BF)
-    send(res_s.at[2], res_r.at[0], "r1", to_x(1))
-    weight_third(1)
-
-    arrived(g_recv, "g")
-
-    def grad_total(b):
-        rows = pl.ds(pl.multiple_of(b * 256, 256), 256)
-        stage[0, rows, :] = (g_own[rows, :] + g_recv[rows, :].astype(F32)).astype(BF)
-
-    loop(2, grad_total)
-    permuted(stage.at[0], gp)
+    res_s[2, 0:256, :] = result_part(2, 0).astype(BF)
+    send(res_s.at[2, 0:256], res_r.at[0, 0:256], "r1a", to_x(1))
+    res_f[0, 0:256, :] = result_part(1, 0)
+    res_f[1, 0:256, :] = result_part(3, 0)
+    left("att0")
+    left("att1")
+    send_grad(0)
+    send_grad(1)
+
+    def result_hand_on_a():
+        arrived(res_a, "ra")
+        res_s[1, 0:256, :] = (res_f[0, 0:256, :] + res_a[...].astype(F32)).astype(BF)
+        send(res_s.at[1, 0:256], res_r.at[1, 0:256], "r3a", to_x(3))
+
+    def result_hand_on_b():
+        arrived(res_b, "rb")
+        res_s[2, 256:512, :] = (res_f[0, 256:512, :] + res_b[...].astype(F32)).astype(BF)
+        send(res_s.at[2, 256:512], res_r.at[0, 256:512], "r1b", to_x(1))
+
+    def result_second():
+        arrived(att_buf.at[1 - q, 256:512], "att1")
+        transposed(1, 1 - q)
+        weight_first(1)
+        res_s[0, 256:512, :] = result_part(0, 1).astype(BF)
+        send(res_s.at[0, 256:512], res_b, "rb", to_x(3))
+        res_s[1, 256:512, :] = result_part(1, 1).astype(BF)
+        send(res_s.at[1, 256:512], res_r.at[1, 256:512], "r3b", to_x(3))
+        res_f[0, 256:512, :] = result_part(2, 1)
+        result_hand_on_a()
+        weight_third(0)
+        weight_second(1)
+        res_f[1, 256:512, :] = result_part(3, 1)
+        result_hand_on_b()
+
+    def grad_total(hp):
+        arrived(g_recv.at[hp], "g%d" % hp)
+        moved = dot(perm[...], (g_own[hp] + g_recv[hp].astype(F32)).astype(BF)).astype(BF)
+        gp[2 * hp] = moved[:, :DH]
+        gp[2 * hp + 1] = moved[:, DH:]
+
+    def grad_cols(h, which):
+        return pl.ds((h // 2) * 512 + which * 256 + (h % 2) * DH, DH)
 
     def backward(level, h):
         n = R >> level
         keys = keys_of(level, h, 0)
         vals = keys_of(level, h, 1)
         grads = chosen(gp[h].astype(F32), level, h)
-        factor = jnp.exp2(mms[level][h] - chosen(m_run[h], level, h)) * chosen(l_run[h], level, h)
-        scaled = grads * factor
+        scaled = grads * mms[level][h]
         delta = jnp.sum(scaled * chosen(attp[h].astype(F32), level, h), axis=1, keepdims=True)
         scaled = scaled.astype(BF)
         e = es[level][h]
@@ -401,78 +447,110 @@
         else:
             dqa[h] += placed(dq, level, h, 0.0)
         scaled_t = dot_t(eye[:DH, :DH], scaled).astype(BF)
-        query_t = dot_t(eye[:DH, :DH], chosen_bf(qp[h], level, h)).astype(BF)
         dv_t = dot(scaled_t, e)
-        dk_t = dot(query_t, ds) * SCALE
+        dk_t = dot(qts[level][h], ds) * SCALE
         both = dot_t(eye[...], jnp.concatenate([dk_t, dv_t], axis=0).astype(BF))
         if level == 0:
             dk0[h] = both[:, :DH]
             dv0[h] = both[:, DH:]
         else:
             shape = snd[level].shape[:-1] + (DH,)
-            snd[level][..., head_cols(h)] = both[:, :DH].astype(BF).reshape(shape)
-            snd[level][..., head_cols(h + HL)] = both[:, DH:].astype(BF).reshape(shape)
+            snd[level][..., grad_cols(h, 0)] = both[:, :DH].astype(BF).reshape(shape)
+            snd[level][..., grad_cols(h, 1)] = both[:, DH:].astype(BF).reshape(shape)
 
     zb = z % 2
-    heads(lambda h: backward(3, h))
-    send(snd3.at[:, 1 - core], cr3, "c3", to_seq(1))
-    heads(lambda h: backward(2, h))
-    send(snd2.at[:, 1 - core], cr2, "c2", to_seq(1))
-    arrived(cr3, "c3")
-    for m in (2, 1, 3):
-        zs3[m - 1] = (snd3[z ^ m, core].astype(F32) + cr3[z ^ m].astype(F32)).astype(BF)
-        send(zs3.at[m - 1], rz3.at[m - 1], "b3_%d" % m, to_seq(2 * m))
-    heads(lambda h: backward(1, h))
-    send(snd1.at[1 - core], cr1, "c1", to_seq(1))
-    arrived(cr2, "c2")
-    zs2[...] = (snd2[zb ^ 1, core].astype(F32) + cr2[zb ^ 1].astype(F32)).astype(BF)
-    send(zs2, rz2, "b2_1", to_seq(2))
+
+    def pair(level, hp):
+        backward(level, 2 * hp)
+        backward(level, 2 * hp + 1)
+
+    def owed_core(level, hp):
+        cols = slice(hp * 512, hp * 512 + 512)
+        if level == 3:
+            send(snd3.at[:, 1 - core, :, cols], cr3.at[:, :, cols], "c3_%d" % hp, to_seq(1))
+        elif level == 2:
+            send(snd2.at[:, 1 - core, :, cols], cr2.at[:, :, cols], "c2_%d" % hp, to_seq(1))
+        else:
+            send(snd1.at[1 - core, :, cols], cr1.at[:, cols], "c1_%d" % hp, to_seq(1))
+
+    def owed_z(level, hp):
+        cols = slice(hp * 512, hp * 512 + 512)
+        if level == 3:
+            arrived(cr3.at[:, :, cols], "c3_%d" % hp)
+            for m in (2, 1, 3):
+                zs3[m - 1, :, cols] = (snd3[z ^ m, core, :, cols].astype(F32) + cr3[z ^ m, :, cols].astype(F32)).astype(BF)
+                send(zs3.at[m - 1, :, cols], rz3.at[m - 1, :, cols], "b3_%d_%d" % (m, hp), to_seq(2 * m))
+        else:
+            arrived(cr2.at[:, :, cols], "c2_%d" % hp)
+            zs2[:, cols] = (snd2[zb ^ 1, core, :, cols].astype(F32) + cr2[zb ^ 1, :, cols].astype(F32)).astype(BF)
+            send(zs2.at[:, cols], rz2.at[:, cols], "b2_1_%d" % hp, to_seq(2))
+
+    result_second()
+    grad_total(0)
+    pair(3, 0)
+    owed_core(3, 0)
+    weight_third(1)
+    pair(2, 0)
+    owed_core(2, 0)
+    owed_z(3, 0)
+    pair(1, 0)
+    owed_core(1, 0)
+    owed_z(2, 0)
+    pair(0, 0)
     weight_fourth(0)
-    heads(lambda h: backward(0, h))
-
-    def natural(dst):
-        def tile(b):
-            rows = pl.ds(pl.multiple_of(b * 256, 256), 256)
-            dst[rows, :] = dot(unperm[rows, :], back[...]).astype(BF)
-
-        loop(2, tile)
-
+    grad_total(1)
+    pair(3, 1)
+    owed_core(3, 1)
+    pair(2, 1)
+    owed_core(2, 1)
+    owed_z(3, 1)
+    pair(1, 1)
+    owed_core(1, 1)
+    owed_z(2, 1)
+    weight_fourth(1)
+    pair(0, 1)
+
+    def natural(dst, hp):
+        cols = slice(hp * 256, hp * 256 + 256)
+        dst[:, cols] = dot(unperm[...], back[:, cols]).astype(BF)
+
+    def key_total(hp):
+        cols_in = slice(hp * 512, hp * 512 + 512)
+        arrived(cr1.at[:, cols_in], "c1_%d" % hp)
+        arrived(rz2.at[:, cols_in], "b2_1_%d" % hp)
+        for m in (1, 3, 2):
+            arrived(rz3.at[m - 1, :, cols_in], "b3_%d_%d" % (m, hp))
+        for which, start_grad, dst in ((0, dk0, dk_o), (1, dv0, dv_o)):
+            for h in (2 * hp, 2 * hp + 1):
+                total = start_grad[h]
+                cols = grad_cols(h, which)
+                owed = snd1[core, :, cols].astype(F32) + cr1[:, cols].astype(F32)
+                total += placed(owed, 1, h, 0.0)
+                owed = snd2[zb, core, :, cols].astype(F32) + cr2[zb, :, cols].astype(F32) + rz2[:, cols].astype(F32)
+                total += placed(owed, 2, h, 0.0)
+                owed = snd3[z, core, :, cols].astype(F32) + cr3[z, :, cols].astype(F32)
+                for m in range(3):
+                    owed += rz3[m, :, cols].astype(F32)
+                total += placed(owed, 3, h, 0.0)
+                back[:, h * DH : (h + 1) * DH] = total.astype(BF)
+            natural(dst, hp)
+
+    key_total(0)
     for h in range(HL):
         back[:, h * DH : (h + 1) * DH] = dqa[h].astype(BF)
-    natural(dq_o)
-
-    arrived(res_r.at[0], "r1")
-    arrived(res_r.at[1], "r3")
+    natural(dq_o, 0)
+    natural(dq_o, 1)
+
+    for rh, name in ((0, "r%da"), (1, "r%db")):
+        arrived(res_r.at[0, rh * 256 : rh * 256 + 256], name % 1)
+        arrived(res_r.at[1, rh * 256 : rh * 256 + 256], name % 3)
 
     def result_total(b):
         rows = pl.ds(pl.multiple_of(b * 128, 128), 128)
-        res_o[rows, :] = (res_f[2, rows, :] + res_r[0, rows, :].astype(F32) + res_r[1, rows, :].astype(F32)).astype(BF)
+        res_o[rows, :] = (res_f[1, rows, :] + res_r[0, rows, :].astype(F32) + res_r[1, rows, :].astype(F32)).astype(BF)
 
     loop(4, result_total)
-    weight_fourth(1)
-
-    arrived(cr1, "c1")
-    for m in (1, 3, 2):
-        arrived(rz3.at[m - 1], "b3_%d" % m)
-    arrived(rz2, "b2_1")
-
-    for which, start_grad, dst in ((0, dk0, dk_o), (1, dv0, dv_o)):
-
-        def key_total(h, which=which, start_grad=start_grad):
-            total = start_grad[h]
-            cols = head_cols(h + HL * which)
-            owed = snd1[core, :, cols].astype(F32) + cr1[:, cols].astype(F32)
-            total += placed(owed, 1, h, 0.0)
-            owed = snd2[zb, core, :, cols].astype(F32) + cr2[zb, :, cols].astype(F32) + rz2[:, cols].astype(F32)
-            total += placed(owed, 2, h, 0.0)
-            owed = snd3[z, core, :, cols].astype(F32) + cr3[z, :, cols].astype(F32)
-            for m in range(3):
-                owed += rz3[m, :, cols].astype(F32)
-            total += placed(owed, 3, h, 0.0)
-            back[:, head_cols(h)] = total.astype(BF)
-
-        heads(key_total)
-        natural(dst)
+    key_total(1)
 
     for source in range(2):
 
@@ -488,7 +566,7 @@
     def _():
         last_hop(0).wait_send()
 
-    for copy in sent:
+    for copy in sent.values():
         copy.wait_send()
 
 
@@ -532,16 +610,17 @@
             f32(HL, R, DH), f32(HL, R, DH), f32(HL, R, DH),
             bf(HL, R, DH), bf(2, R, C), bf(2, C, R),
             bf(4, R, C), bf(2, C, 2048),
-            f32(R, C), bf(R, C), bf(R, C), bf(HL, R, DH),
-            bf(3, R, C), bf(256, C), bf(256, C), bf(2, R, C), f32(3, R, C),
+            f32(2, R, 256), bf(2, R, 256), bf(2, R, 256), bf(HL, R, DH),
+            bf(3, R, C), bf(256, C), bf(256, C), bf(2, R, C), f32(2, R, C),
             bf(2, 4, C, 256), bf(2, 4, C, 256),
-            bf(2, 3, C, 256), bf(2, 256, 256), bf(2, 256, 256), bf(2, 2, C, 256), f32(2, 3, C, 256),
+            bf(2, 3, C, 256), bf(2, 256, 256), bf(2, 256, 256), bf(2, 2, C, 256), f32(2, 2, 256, 256), f32(2, C, 256),
             bf(2, 512, 256), bf(2, 512, 256),
             f32(HL, R, DH), f32(HL, R, DH), f32(HL, R, DH),
             bf(2, 256, 1024), bf(2, 2, 128, 1024), bf(4, 2, 64, 1024),
             bf(256, 1024), bf(2, 128, 1024), bf(4, 64, 1024),
             bf(128, 1024), bf(3, 64, 1024), bf(128, 1024), bf(3, 64, 1024),
             bf(R, C),
+            bf(HL, DH, 512), bf(HL, DH, 256), bf(HL, DH, 128), bf(HL, DH, 64),
             pltpu.SemaphoreType.DMA((count,)), pltpu.SemaphoreType.DMA((count,)), pltpu.SemaphoreType.DMA((5,)),
         ],
         compiler_params=pltpu.CompilerParams(

time: 78.4 us -> 73.7 us (0.940)
  Pallas kernels: 77.2 us -> 72.7 us
    pallas_call x1, Pallas kernels: 74.7 us -> 70.2 us  [shards(): pl.pallas_call(kernel, out_shape=outs, in_specs=[pl.BlockSpec(memory_spac...]
where the time goes in v1:
time: 73.7 us; the launch traced here: 73.5 us
  Pallas kernels  72.7 us (99%)
  between operations  0.82 us (1%)
    pallas_call x1, Pallas kernels, shards(): pl.pallas_call(kernel, out_shape=outs, in_specs=[pl.BlockSpec(memory_spac...  70.2 us
    pallas_call x1, Pallas kernels, shards(): pl.pallas_call(hand_over, out_shape=outs, in_specs=[any_spec] * 5, out_sp...  2.52 us

profile of v1, /device:TPU:8, one launch (start us, length us, event | category | flops | bytes accessed | tf_op | source)
XLA Modules:
  0.0 73.5 jit_solution(4298645142220730231)
XLA Ops:
  0.6 70.2 %shard_map.101 = (bf16[512,512]{1,0:T(8,128)(2,1)}, bf16[512,512]{1,0:T(8,128)(2,1)}, bf16[512,512]{1,0:T(8,128)(2,1)}, bf16[512,512]{1,0:T(8,128)(2,1)}, bf16[512,256]{1,0:T(8,128)(2,1)}) custom-call(s32[3,32]{1,0:T(4,128)} %offs.1, bf16[512,512]{1,0:T(8,128)(2,1)} %q_hbm.1, bf16[512,512]{1,0:T(8,128)(2,1)} %k_hbm.1, bf16[512,512]{1,0:T(8,128)(2,1)} %v_hbm.1, ...), custom_call_target="tpu_custom_call" | custom-call | tf_op jit(solution)/shard_map/pallas_call | solution.py:599
  70.8 2.5 %shard_map.102 = (bf16[512,512]{1,0:T(8,128)(2,1)}, bf16[512,512]{1,0:T(8,128)(2,1)}, bf16[512,512]{1,0:T(8,128)(2,1)}, bf16[512,512]{1,0:T(8,128)(2,1)}, bf16[512,256]{1,0:T(8,128)(2,1)}) custom-call(bf16[512,512]{1,0:T(8,128)(2,1)} %get-tuple-element.10.refs_0_, bf16[512,512]{1,0:T(8,128)(2,1)} %get-tuple-element.11.refs_1_, ...), custom_call_target="tpu_custom_call" | custom-call | tf_op jit(solution)/shard_map/pallas_call | solution.py:630

commit v2 on v1

--- a/solution.py
+++ b/solution.py
@@ -52,6 +52,7 @@
 
 def kernel(
     offs, q_hbm, k_hbm, v_hbm, w_hbm, og_hbm,
+    res_out, dq_out, dk_out, dv_out, gw_out,
     res_o, dq_o, dk_o, dv_o, gw_o,
     stage, perm, unperm, eye, qp, kp, vp, kv1, kv2, kv3, e0, e1, e2, e3, mm0, mm1, mm2, mm3,
     m_run, l_run, n_run, attp, att_buf, att_t, og_buf, wblk, g_own, g_send, g_recv, gp,
@@ -449,7 +450,7 @@
         scaled_t = dot_t(eye[:DH, :DH], scaled).astype(BF)
         dv_t = dot(scaled_t, e)
         dk_t = dot(qts[level][h], ds) * SCALE
-        both = dot_t(eye[...], jnp.concatenate([dk_t, dv_t], axis=0).astype(BF))
+        both = jnp.transpose(jnp.concatenate([dk_t, dv_t], axis=0))
         if level == 0:
             dk0[h] = both[:, :DH]
             dv0[h] = both[:, DH:]
@@ -540,6 +541,7 @@
         back[:, h * DH : (h + 1) * DH] = dqa[h].astype(BF)
     natural(dq_o, 0)
     natural(dq_o, 1)
+    written = [local(dq_o, dq_out, 5)]
 
     for rh, name in ((0, "r%da"), (1, "r%db")):
         arrived(res_r.at[0, rh * 256 : rh * 256 + 256], name % 1)
@@ -550,7 +552,10 @@
         res_o[rows, :] = (res_f[1, rows, :] + res_r[0, rows, :].astype(F32) + res_r[1, rows, :].astype(F32)).astype(BF)
 
     loop(4, result_total)
+    written.append(local(res_o, res_out, 6))
     key_total(1)
+    written.append(local(dk_o, dk_out, 7))
+    written.append(local(dv_o, dv_out, 8))
 
     for source in range(2):
 
@@ -559,6 +564,7 @@
             arrived(gy_r.at[source], "y%d" % source)
 
     gw_o[...] = (gy_r[0].astype(F32) + gy_r[1].astype(F32)).astype(BF)
+    written.append(local(gw_o, gw_out, 9))
 
     last_hop(1).wait_send()
 
@@ -568,6 +574,8 @@
 
     for copy in sent.values():
         copy.wait_send()
+    for copy in written:
+        copy.wait()
 
 
 def hand_over(*refs):
@@ -586,7 +594,6 @@
 def shards(queries, keys, values, offsets, out_weight, out_grad):
     wide = jax.ShapeDtypeStruct((R, C), BF)
     any_spec = pl.BlockSpec(memory_space=pl.ANY)
-    vmem = pl.BlockSpec(memory_space=pltpu.VMEM)
 
     def bf(*shape):
         return pltpu.VMEM(shape, BF)
@@ -600,8 +607,9 @@
         kernel,
         out_shape=outs,
         in_specs=[pl.BlockSpec(memory_space=pltpu.SMEM)] + [any_spec] * 5,
-        out_specs=[vmem] * 5,
+        out_specs=[any_spec] * 5,
         scratch_shapes=[
+            bf(R, C), bf(R, C), bf(R, C), bf(R, C), bf(512, 256),
             bf(3, R, C), bf(R, R), bf(R, R), bf(R, R),
             bf(HL, R, DH), bf(HL, R, DH), bf(HL, R, DH),
             bf(2, 256, 1024), bf(4, 128, 1024), bf(8, 64, 1024),
@@ -621,7 +629,7 @@
             bf(128, 1024), bf(3, 64, 1024), bf(128, 1024), bf(3, 64, 1024),
             bf(R, C),
             bf(HL, DH, 512), bf(HL, DH, 256), bf(HL, DH, 128), bf(HL, DH, 64),
-            pltpu.SemaphoreType.DMA((count,)), pltpu.SemaphoreType.DMA((count,)), pltpu.SemaphoreType.DMA((5,)),
+            pltpu.SemaphoreType.DMA((count,)), pltpu.SemaphoreType.DMA((count,)), pltpu.SemaphoreType.DMA((12,)),
         ],
         compiler_params=pltpu.CompilerParams(
             collective_id=0, has_side_effects=True, vmem_limit_bytes=60 * 1024 * 1024

time: 73.7 us -> 70.7 us (0.959)
  Pallas kernels: 72.7 us -> 69.8 us
    pallas_call x1, Pallas kernels: 70.2 us -> 67.3 us  [shards(): pl.pallas_call(kernel, out_shape=outs, in_specs=[pl.BlockSpec(memory_spac...]
where the time goes in v2:
time: 70.7 us; the launch traced here: 70.6 us
  Pallas kernels  69.8 us (99%)
  between operations  0.8 us (1%)
    pallas_call x1, Pallas kernels, shards(): pl.pallas_call(kernel, out_shape=outs, in_specs=[pl.BlockSpec(memory_spac...  67.3 us
    pallas_call x1, Pallas kernels, shards(): pl.pallas_call(hand_over, out_shape=outs, in_specs=[any_spec] * 5, out_sp...  2.52 us

profile of v2, /device:TPU:8, one launch (start us, length us, event | category | flops | bytes accessed | tf_op | source)
XLA Modules:
  0.0 70.6 jit_solution(14194372375502818550)
XLA Ops:
  0.6 67.3 %shard_map.101 = (bf16[512,512]{1,0:T(8,128)(2,1)}, bf16[512,512]{1,0:T(8,128)(2,1)}, bf16[512,512]{1,0:T(8,128)(2,1)}, bf16[512,512]{1,0:T(8,128)(2,1)}, bf16[512,256]{1,0:T(8,128)(2,1)}) custom-call(s32[3,32]{1,0:T(4,128)} %offs.1, bf16[512,512]{1,0:T(8,128)(2,1)} %q_hbm.1, bf16[512,512]{1,0:T(8,128)(2,1)} %k_hbm.1, bf16[512,512]{1,0:T(8,128)(2,1)} %v_hbm.1, ...), custom_call_target="tpu_custom_call" | custom-call | tf_op jit(solution)/shard_map/pallas_call | solution.py:606
  67.9 2.5 %shard_map.102 = (bf16[512,512]{1,0:T(8,128)(2,1)}, bf16[512,512]{1,0:T(8,128)(2,1)}, bf16[512,512]{1,0:T(8,128)(2,1)}, bf16[512,512]{1,0:T(8,128)(2,1)}, bf16[512,256]{1,0:T(8,128)(2,1)}) custom-call(bf16[512,512]{1,0:T(8,128)(2,1)} %get-tuple-element.10.refs_0_, bf16[512,512]{1,0:T(8,128)(2,1)} %get-tuple-element.11.refs_1_, ...), custom_call_target="tpu_custom_call" | custom-call | tf_op jit(solution)/shard_map/pallas_call | solution.py:638
